TPU v7x, 256 devices: a whole 4x4x8 slice. The times are simulated.
256 devices in a mesh: aux: 4 (over y), bas: 64 (over x, z, core).
Axes of the slice: x: 4, y: 4, z: 8, core: 2. Of those that a mesh axis runs over, the one named last changes fastest.
Arguments:
- integrals: bfloat16 [8, 128, 32, 128, 128], P('aux', 'bas'), may hold values from -6 to 6
- orbitals: bfloat16 [16384, 10240], P('bas'), may hold values from -0.015625 to 0.015625
- screen_list: int32 [128, 32], P('bas'), may hold values from 0 to 127, as said below
- screen_count: int32 [128], P('bas'), may hold values from 16 to 32
- domains: int32 [128, 6], P('bas'), may hold values from 0 to 79, as said below
- pair_list: int32 [128, 4], P('bas'), may hold values from 0 to 127, as said below
Outputs:
- exchange_tiles: bfloat16 [128, 4, 128, 128], P('bas')
Inputs may be any that keep to these rules, and one draw needn't show every extreme that they name: `screen_list`: the tiles of one row are distinct; among the 64 entries of the rows of one index of bas, at most 1 name tiles held by any one index of bas, and that many in every draw. `domains`: the 6 entries of a row are distinct. `pair_list`: each entry lies within 2 tiles of its row's own tile.
All inputs are finite; a program needn't handle non-finite values.
Results may differ from a plain program's by a relative error of at most 0.0032.
Values may be sent and summed in bfloat16 or wider, within the bound.
A program may use at most 128 MiB of HBM per device.

v0:
```python
import jax
import jax.numpy as jnp
from jax import lax
from jax.sharding import PartitionSpec as P


def with_halo(shard, sides, width):
    for axis, dim in sides:
        size, length = (lax.axis_size(axis), shard.shape[dim])
        up = [(i, (i + 1) % size) for i in range(size - 1)]
        down = [(j, i) for i, j in up]
        last = lax.slice_in_dim(shard, length - width, length, axis=dim)
        first = lax.slice_in_dim(shard, 0, width, axis=dim)
        before = lax.ppermute(last, axis, up)
        after = lax.ppermute(first, axis, down)
        shard = jnp.concatenate([before, shard, after], axis=dim)
    return shard


def plan_slots(wanted_tiles, tile_count, capacity):
    wanted = wanted_tiles.reshape(-1)
    holder = wanted // tile_count
    request_ids = jnp.arange(wanted.shape[0])
    shared = holder[:, None] == holder[None, :]
    earlier = request_ids[None, :] < request_ids[:, None]
    order_in = jnp.sum((shared & earlier).astype(jnp.int32), axis=1)
    return (wanted, holder * capacity + order_in)


def record_table(onehot, within_tile, wanted_domains):
    filled = jnp.sum(onehot, axis=0)
    local_tile = jnp.sum(onehot * within_tile[:, None], axis=0) + filled - 1
    blocks = jnp.sum(onehot[:, :, None] * wanted_domains[:, None, :], axis=0)
    return jnp.concatenate([local_tile[:, None], blocks], axis=1)


def on_device(integrals, orbitals, screen_list, screen_count, domains, pair_list):
    bas_count = lax.axis_size("bas")
    position = lax.axis_index("bas")
    tile_count, slot_count = screen_list.shape
    dom_blocks = domains.shape[1]
    pair_count = pair_list.shape[1]
    tile_width = integrals.shape[-1]
    occ_blocks = orbitals.shape[1] // tile_width
    capacity = (tile_count * slot_count + bas_count - 1) // bas_count
    wanted, slot_of = plan_slots(screen_list, tile_count, capacity)
    all_lists, all_domains = (
        lax.all_gather(screen_list, "bas", axis=0, tiled=True),
        lax.all_gather(domains, "bas", axis=0, tiled=True),
    )

    def for_source(source_lists, source_domains):
        source_wanted, source_slots = plan_slots(source_lists, tile_count, capacity)
        source_rows = jnp.repeat(source_domains, slot_count, axis=0)
        targets = position * capacity + jnp.arange(capacity)
        onehot = (source_slots[:, None] == targets[None, :]).astype(jnp.int32)
        return record_table(onehot, source_wanted % tile_count, source_rows)

    records = jax.vmap(for_source)(
        all_lists.reshape(bas_count, tile_count, slot_count),
        all_domains.reshape(bas_count, tile_count, dom_blocks),
    )
    blocked = orbitals.reshape(tile_count, tile_width, occ_blocks, tile_width)
    flat_records = records.reshape(bas_count * capacity, 1 + dom_blocks)
    local_tile = flat_records[:, 0]
    picked = blocked[jnp.maximum(local_tile, 0)[:, None], :, flat_records[:, 1:], :]
    picked = jnp.where((local_tile >= 0)[:, None, None, None], picked, jnp.zeros((), picked.dtype))
    picked = picked.reshape(bas_count, capacity, dom_blocks, -1, tile_width)
    answers = lax.all_to_all(picked, "bas", split_axis=0, concat_axis=0, tiled=True)
    fetched = answers.reshape(bas_count * capacity, dom_blocks, tile_width, tile_width)[slot_of]
    fetched = fetched.reshape(tile_count, slot_count, dom_blocks, tile_width, tile_width)
    active = (jnp.arange(slot_count)[None, :] < screen_count[:, None]).astype(fetched.dtype)
    fetched = fetched * active[:, :, None, None, None]
    halfway = jnp.einsum(
        "pmsab,msdbo->mapdo", integrals, fetched, preferred_element_type=jnp.float32
    ).astype(jnp.bfloat16)
    aux_count = halfway.shape[2]
    flat_half = halfway.reshape(tile_count, tile_width, -1)
    rim_half, rim_domains = (
        with_halo(flat_half, (("bas", 0),), tile_count),
        with_halo(domains, (("bas", 0),), tile_count),
    )
    partner_row = pair_list - (position * tile_count - tile_count)
    partner_half = rim_half[partner_row].reshape(
        tile_count, pair_count, tile_width, aux_count, dom_blocks, tile_width
    )
    partner_dom = rim_domains[partner_row]
    intersection = (domains[:, None, :, None] == partner_dom[:, :, None, :]).astype(jnp.bfloat16)
    aligned = jnp.einsum(
        "mkde,mkbpeo->mkbpdo", intersection, partner_half, preferred_element_type=jnp.float32
    ).astype(jnp.bfloat16)
    partial_value = jnp.einsum(
        "mapdo,mkbpdo->mkab", halfway, aligned, preferred_element_type=jnp.float32
    )
    summed = lax.psum(partial_value, "aux")
    return summed.astype(jnp.bfloat16)


def solution(mesh):
    in_specs = (
        P("aux", "bas", None, None, None),
        P("bas", None),
        P("bas", None),
        P("bas"),
        P("bas", None),
        P("bas", None),
    )
    out_specs = P("bas", None, None, None)
    return jax.shard_map(
        on_device, mesh=mesh, in_specs=in_specs, out_specs=out_specs, check_vma=False
    )
```

profile of v0, /device:TPU:1, one launch (start us, length us, event | category | flops | bytes accessed | tf_op | source)
XLA Modules:
  0.0 492.1 jit_solution(18370515818697701980)
XLA Ops:
  0.0 48.2 %all-gather = s32[64,2,32]{2,1,0:T(2,128)S(1)} all-gather(s32[1,2,32]{2,1,0:T(2,128)} %bitcast.98), channel_id=1, replica_groups=mesh['aux'=4,'bas'=64] {'bas'}, dimensions={0}, use_global_device_ids=true | all-gather | bytes 16640 | tf_op jit(solution)/shard_map/all_gather | solution.py:48
  48.4 1.9 convert_reduce_fusion
  50.4 0.2 convert_reduce_fusion.1
  50.6 0.1 reduce_sum.70
  50.7 0.1 reduce_sum.73
  51.1 42.7 %all-gather.1 = s32[64,2,6]{2,1,0:T(2,128)S(1)} all-gather(s32[1,2,6]{2,1,0:T(2,128)} %bitcast.95), channel_id=1, replica_groups=mesh['aux'=4,'bas'=64] {'bas'}, dimensions={0}, use_global_device_ids=true | all-gather | bytes 3120 | tf_op jit(solution)/shard_map/all_gather | solution.py:49
  94.1 0.1 reshape.355
  94.3 3.7 copy.85
  98.0 3.7 copy.64
  101.7 18.9 %gather_fusion = bf16[384,128,128]{2,1,0:T(8,128)(2,1)} fusion(bf16[2,128,80,128]{3,1,2,0:T(8,128)(2,1)} %copy.64, s32[384]{0:T(512)S(1)} %reshape.355), kind=kCustom, calls=%fused_computation | custom fusion | bytes 25168896 | tf_op jit(solution)/shard_map/gather | solution.py:66
  120.6 10.8 %select_bitcast_fusion = bf16[64,1,6,128,128]{4,3,2,1,0:T(8,128)(2,1)} fusion(bf16[64,1,6,128,128]{4,3,2,0,1:T(8,128)(2,1)} %bitcast.84, pred[64]{0:T(512)(128)(4,1)S(1)} %compare_bitcast_fusion), kind=kLoop, calls=%fused_computation.7 | loop fusion | flops 6291456 | bytes 25165888 | tf_op jit(solution)/shard_map/jit(_where)/select_n | solution.py:67
  131.3 6.3 %all-to-all-start = ((bf16[64,1,6,128,128]{4,3,2,1,0:T(8,128)(2,1)}), bf16[64,1,6,128,128]{4,3,2,1,0:T(8,128)(2,1)}, u32[]{:S(2)}, u32[]{:S(2)}) async-start(bf16[64,1,6,128,128]{4,3,2,1,0:T(8,128)(2,1)} %select_bitcast_fusion), calls=%async_computation | async-start | bytes 25165824 | tf_op jit(solution)/shard_map/all_to_all | solution.py:69
  137.9 0.2 convert_reduce_fusion.2
  138.2 275.2 %all-to-all-done = bf16[64,1,6,128,128]{4,3,2,1,0:T(8,128)(2,1)} async-done(((bf16[64,1,6,128,128]{4,3,2,1,0:T(8,128)(2,1)}), bf16[64,1,6,128,128]{4,3,2,1,0:T(8,128)(2,1)}, u32[]{:S(2)}, u32[]{:S(2)}) %all-to-all-start) | async-done | bytes 12582944 | tf_op jit(solution)/shard_map/all_to_all | solution.py:69
  413.3 11.8 %gather_fusion.1 = bf16[64,6,128,128]{3,2,1,0:T(8,128)(2,1)} fusion(bf16[64,6,128,128]{3,2,1,0:T(8,128)(2,1)} %bitcast.13, s32[1024]{0:T(1024)S(1)} %pad_clamp_fusion.1), kind=kCustom, calls=%fused_computation.1 | custom fusion | bytes 25166080 | tf_op jit(solution)/shard_map/gather | solution.py:70
  425.2 11.9 %bitcast_convert_fusion = bf16[2,6,128,2,128]{4,2,3,1,0:T(8,128)(2,1)S(1)} fusion(bf16[2,32,6,128,128]{4,3,2,1,0:T(8,128)(2,1)} %bitcast.87, bf16[2,32]{1,0:T(2,128)(2,1)S(1)} %compare_convert_fusion, bf16[2,2,32,128,128]{4,3,2,1,0:T(8,128)(2,1)} %param.6), kind=kOutput, calls=%fused_computation.14 | convolution fusion | flops 3227910144 | bytes 17563776 | tf_op jit(solution)/shard_map/pmsab,msdbo->mapdo/dot_general | solution.py:74
  437.1 0.8 copy-done.1
  437.9 1.9 collective-permute-start
  439.8 2.5 collective-permute-start.1
  442.3 3.1 collective-permute-start.2
  445.4 1.9 collective-permute-start.3
  447.5 1.3 collective-permute-done.2
  448.8 4.5 collective-permute-done.3
  453.3 0.6 gather_fusion.3
  453.9 0.9 copy-done
  454.8 1.6 pad_maximum_fusion
  456.4 2.6 gather_fusion.2
  459.0 7.6 %copy.69 = bf16[2,4,128,2,6,128]{5,4,3,2,1,0:T(8,128)(2,1)} copy(bf16[2,4,128,2,6,128]{2,5,4,3,1,0:T(8,128)(2,1)} %bitcast.86) | data formatting | bytes 6291456 | tf_op jit(solution)/shard_map/reshape | solution.py:84
  466.6 3.6 convert_bitcast_fusion
  470.2 1.1 fusion.9
  471.3 20.0 %all-reduce.1 = bf16[2,4,128,128]{2,3,1,0:T(8,128)(2,1)S(1)} all-reduce(f32[2,4,128,128]{2,3,1,0:T(8,128)S(1)} %fusion.9), channel_id=1, replica_groups=mesh['aux'=4,'bas'=64] {'aux'}, use_global_device_ids=true, to_apply=%region_7.8 | all-reduce | flops 131072 | bytes 786432 | tf_op jit(solution)/shard_map/psum | solution.py:95
  491.3 0.9 copy.72
  (42 shorter events, 1.3 us)
Async XLA Ops:
  131.3 6.3 %copy-start.4 = (s32[2,32]{1,0:T(2,128)S(1)}, s32[2,32]{1,0:T(2,128)}, u32[]{:S(2)}) copy-start(s32[2,32]{1,0:T(2,128)} %param.8) | copy-start | bytes 772
  131.3 6.7 %copy-start.6 = (s32[2]{0:T(128)S(1)}, s32[2]{0:T(128)}, u32[]{:S(2)}) copy-start(s32[2]{0:T(128)} %param.9) | copy-start | bytes 28
  131.3 282.0 %all-to-all-start = ((bf16[64,1,6,128,128]{4,3,2,1,0:T(8,128)(2,1)}), bf16[64,1,6,128,128]{4,3,2,1,0:T(8,128)(2,1)}, u32[]{:S(2)}, u32[]{:S(2)}) async-start(bf16[64,1,6,128,128]{4,3,2,1,0:T(8,128)(2,1)} %select_bitcast_fusion), calls=%async_computation | async-start | bytes 25165824 | tf_op jit(solution)/shard_map/all_to_all | solution.py:69
  425.2 17.1 %copy-start.3 = (s32[2,6]{1,0:T(2,128)S(1)}, s32[2,6]{1,0:T(2,128)}, u32[]{:S(2)}) copy-start(s32[2,6]{1,0:T(2,128)} %param.10) | copy-start | bytes 148
  425.2 22.2 %copy-start.5 = (s32[2,4]{1,0:T(2,128)S(1)}, s32[2,4]{1,0:T(2,128)}, u32[]{:S(2)}) copy-start(s32[2,4]{1,0:T(2,128)} %param.11) | copy-start | bytes 100
  437.1 0.9 copy-start.1
  437.9 15.9 %collective-permute-start = (bf16[2,128,1536]{1,2,0:T(8,128)(2,1)S(1)}, bf16[2,128,1536]{1,2,0:T(8,128)(2,1)S(1)}, u32[]{:S(2)}, u32[]{:S(2)}) collective-permute-start(bf16[2,128,1536]{1,2,0:T(8,128)(2,1)S(1)} %bitcast.89), channel_id=1, source_target_pairs={{0,1},{1,2},{2,3},{3,4},{4,5},{5,6},{6,7},{7,8},{8,9},{9,10},{10,1... | collective-permute-start | bytes 2359304 | tf_op jit(solution)/shard_map/ppermute | solution.py:14
  439.8 14.9 %collective-permute-start.1 = (bf16[2,128,1536]{1,2,0:T(8,128)(2,1)S(1)}, bf16[2,128,1536]{1,2,0:T(8,128)(2,1)}, u32[]{:S(2)}, u32[]{:S(2)}) collective-permute-start(bf16[2,128,1536]{1,2,0:T(8,128)(2,1)S(1)} %bitcast.90), channel_id=1, source_target_pairs={{1,0},{2,1},{3,2},{4,3},{5,4},{6,5},{7,6},{8,7},{9,8},{10,9},{11,1... | collective-permute-start | bytes 2359304 | tf_op jit(solution)/shard_map/ppermute | solution.py:15
  442.3 6.5 %collective-permute-start.2 = (s32[2,6]{1,0:T(2,128)S(1)}, s32[2,6]{1,0:T(2,128)S(1)}, u32[]{:S(2)}, u32[]{:S(2)}) collective-permute-start(s32[2,6]{1,0:T(2,128)S(1)} %copy-done.3), channel_id=1, source_target_pairs={{0,1},{1,2},{2,3},{3,4},{4,5},{5,6},{6,7},{7,8},{8,9},{9,10},{10,1... | collective-permute-start | bytes 152 | tf_op jit(solution)/shard_map/ppermute | solution.py:14
  445.4 7.8 %collective-permute-start.3 = (s32[2,6]{1,0:T(2,128)S(1)}, s32[2,6]{1,0:T(2,128)S(1)}, u32[]{:S(2)}, u32[]{:S(2)}) collective-permute-start(s32[2,6]{1,0:T(2,128)S(1)} %copy-done.3), channel_id=1, source_target_pairs={{1,0},{2,1},{3,2},{4,3},{5,4},{6,5},{7,6},{8,7},{9,8},{10,9},{11,1... | collective-permute-start | bytes 152 | tf_op jit(solution)/shard_map/ppermute | solution.py:15
  453.8 0.9 copy-start
  466.6 3.6 copy-start.2
where the time goes:
time: 496 us; the launch traced here: 492 us
  waiting for transfers between devices  281 us (57%)
  blocking collectives  111 us (22%)
  local copies, waits for them, and re-layouts  52.7 us (11%)
  matrix products  16.5 us (3%)
  starting transfers between devices  15.7 us (3%)
  other arithmetic  15.1 us (3%)
    all_to_all x1, waiting for transfers between devices, on_device(): lax.all_to_all(picked, 'bas', split_axis=0, concat_axis=0, tiled=True)  275 us
    all_gather x1, blocking collectives, on_device(): lax.all_gather(screen_list, 'bas', axis=0, tiled=True)  48.2 us
    all_gather x1, blocking collectives, on_device(): lax.all_gather(domains, 'bas', axis=0, tiled=True)  42.7 us
    psum x1, blocking collectives, on_device(): summed = lax.psum(partial_value, 'aux')  20 us
    gather x1, local copies, waits for them, and re-layouts, on_device(): blocked[jnp.maximum(local_tile, 0)[:, None], :, flat_records[:, 1:], :]  18.9 us
    dot_general x1, matrix products, on_device(): jnp.einsum('pmsab,msdbo->mapdo', integrals, fetched, preferred_element_ty...  11.9 us
    gather x1, local copies, waits for them, and re-layouts, on_device(): answers.reshape(bas_count * capacity, dom_blocks, tile_width, tile_width)  11.8 us
    select_n x1, other arithmetic, on_device(): jnp.where((local_tile >= 0)[:, None, None, None], picked, jnp.zeros((), p...  10.8 us
  transfers between devices with their start and end apart: 5, of which 3 were waited for; matrix products, arithmetic and copies ran while one was open for 0% of the time, Pallas kernels for 0%

commit v1 on v0

v1 whole, which is shorter than its diff:
```python
import functools

import jax
import jax.numpy as jnp
from jax import lax
from jax.experimental import pallas as pl
from jax.experimental.pallas import tpu as pltpu
from jax.sharding import PartitionSpec as P

MESH = pl.DeviceIdType.MESH
TW = 128
DOM = 6
DIRECT = 16
HALF = 2 * DIRECT
ROWS = 4 * TW
LANE_TILE, LANE_DOM, LANE_SLOT, LANE_ROW, LANE_ON = 0, 1, 7, 8, 9


def kernel(
    lists_ref, count_ref, dom_ref, pair_ref, integrals_ref, orbitals_ref, out_ref,
    ints, orbs, rec, rec_s, req, req_s, domv, dom_s, match_s,
    sent, rhs, ints_out, ints_in, lhs, own, other, other_in, halo, tiles, tiles_in, result,
    load_sem, rec_send, rec_recv, dom_send, dom_recv,
    block_send, block_recv, pass_send, pass_recv, ints_sem,
    part_send, part_recv, halo_send, halo_recv, tile_send, tile_recv, res_send, res_recv,
):
    y, bas = lax.axis_index("aux"), lax.axis_index("bas")
    x, z, c = bas // 16, (bas // 2) % 8, bas % 2
    y0, y1 = y % 2, y // 2
    partner, mate = y + 1 - 2 * y0, 3 - y
    before, after = (bas + 63) % 64, (bas + 1) % 64

    def place(px, pz, pc):
        return (((px + 8) % 4) * 8 + (pz + 16) % 8) * 2 + pc

    def target(i):
        return place(x - i // 4, z - 2 * (i % 4) - (c + y0) % 2, (y0 + y1 + c) % 2)

    def holder(plane0, plane1, i):
        return place(x + i // 4, z + 2 * (i % 4) + (c + plane1) % 2, (plane0 + plane1 + c) % 2)

    def half_holder(plane0, j):
        q = j // DIRECT
        return holder((plane0 + q) % 2, (y1 + q) % 2, j % DIRECT)

    load_ints = pltpu.make_async_copy(integrals_ref, ints, load_sem.at[0])
    load_orbs = pltpu.make_async_copy(orbitals_ref, orbs, load_sem.at[1])
    load_ints.start()
    load_orbs.start()

    barrier = pltpu.get_barrier_semaphore()

    def greet(device):
        pl.semaphore_signal(barrier, inc=1, device_id=device, device_id_type=MESH)

    @pl.loop(0, DIRECT)
    def _(i):
        @pl.when(target(i) != bas)
        def _():
            greet({"bas": target(i)})

        @pl.when(holder(y0, y1, i) != bas)
        def _():
            greet({"bas": holder(y0, y1, i)})

    for r in range(1, 4):
        greet({"aux": (y + r) % 4})
    greet({"bas": before})
    greet({"bas": after})

    holder_ids = lax.broadcasted_iota(jnp.int32, (64, 32), 0)
    slot_ids = lax.broadcasted_iota(jnp.int32, (64, 32), 1)
    lanes = lax.broadcasted_iota(jnp.int32, (64, TW), 1)
    table = jnp.zeros((64, TW), jnp.int32)
    for m in range(2):
        row = lists_ref[m : m + 1, :]
        hit = (row >> 1) == holder_ids
        found = jnp.sum(jnp.where(hit, 1, 0), axis=1, keepdims=True)
        tile = jnp.sum(jnp.where(hit, row & 1, 0), axis=1, keepdims=True)
        slot = jnp.sum(jnp.where(hit, slot_ids, 0), axis=1, keepdims=True)
        on = found * jnp.where(slot < count_ref[m], 1, 0)
        table += jnp.where(lanes == LANE_TILE, tile, 0)
        table += jnp.where(lanes == LANE_SLOT, slot + found * (32 * m), 0)
        table += jnp.where(lanes == LANE_ROW, found * m, 0)
        table += jnp.where(lanes == LANE_ON, on, 0)
        for d in range(DOM):
            table += jnp.where(lanes == LANE_DOM + d, found * dom_ref[m, d], 0)
    rec[...] = jnp.clip(table, 0, 79)
    lane = lax.broadcasted_iota(jnp.int32, (8, TW), 1)
    mine = jnp.zeros((8, TW), jnp.int32)
    for m in range(2):
        for d in range(DOM):
            mine += jnp.where(lane == m * DOM + d, dom_ref[m, d], 0)
    domv[1] = mine
    rec_local = pltpu.make_async_copy(rec, rec_s, load_sem.at[2])
    rec_local.start()

    alone = ((y0 + y1 + 1) % 2) * ((c + y0 + 1) % 2)
    pl.semaphore_wait(barrier, 2 * DIRECT + 5 - 2 * alone)

    def rec_copy(i):
        return pltpu.make_async_remote_copy(
            src_ref=rec.at[pl.ds(holder(y0, y1, i), 1), :], dst_ref=req.at[pl.ds(i, 1), :],
            send_sem=rec_send.at[i], recv_sem=rec_recv.at[i],
            device_id={"bas": holder(y0, y1, i)}, device_id_type=MESH,
        )

    def rec_self(i):
        return pltpu.make_async_copy(
            rec.at[pl.ds(holder(y0, y1, i), 1), :], req.at[pl.ds(i, 1), :], rec_recv.at[i]
        )

    @pl.loop(0, DIRECT)
    def _(i):
        @pl.when(holder(y0, y1, i) != bas)
        def _():
            rec_copy(i).start()

        @pl.when(holder(y0, y1, i) == bas)
        def _():
            rec_self(i).start()

    def dom_copy(way):
        return pltpu.make_async_remote_copy(
            src_ref=domv.at[1], dst_ref=domv.at[2 - 2 * way],
            send_sem=dom_send.at[way], recv_sem=dom_recv.at[way],
            device_id={"bas": after if way else before}, device_id_type=MESH,
        )

    dom_copy(0).start()
    dom_copy(1).start()

    def slot_of(at):
        return jnp.minimum(rec_s[at, LANE_SLOT], 63)

    rec_local.wait()
    load_ints.wait()

    @pl.loop(0, HALF)
    def _(j):
        slot = slot_of(half_holder((y0 + 1) % 2, j))
        for p in range(2):
            ints_out[j, p] = ints[p, slot]

    ints_copy = pltpu.make_async_remote_copy(
        src_ref=ints_out, dst_ref=ints_in, send_sem=ints_sem.at[0], recv_sem=ints_sem.at[1],
        device_id={"aux": partner}, device_id_type=MESH,
    )
    ints_copy.start()

    @pl.loop(0, DIRECT)
    def _(i):
        rec_self(i).wait()

    req_local = pltpu.make_async_copy(req, req_s, load_sem.at[3])
    req_local.start()
    req_local.wait()
    load_orbs.wait()

    def rows_of(i):
        return pl.ds(pl.multiple_of(i * TW, TW), TW)

    def block_copy(g, i):
        return pltpu.make_async_remote_copy(
            src_ref=sent.at[g, i], dst_ref=rhs.at[g, rows_of(i), :],
            send_sem=block_send.at[g, i], recv_sem=block_recv.at[g, i],
            device_id={"bas": target(i)}, device_id_type=MESH,
        )

    def block_self(g, i):
        return pltpu.make_async_copy(sent.at[g, i], rhs.at[g, rows_of(i), :], block_recv.at[g, i])

    def pass_copy(g, i):
        return pltpu.make_async_remote_copy(
            src_ref=rhs.at[g, rows_of(i), :], dst_ref=rhs.at[g, rows_of(DIRECT + i), :],
            send_sem=pass_send.at[g], recv_sem=pass_recv.at[g],
            device_id={"aux": mate}, device_id_type=MESH,
        )

    @pl.loop(0, DOM * DIRECT)
    def _(t):
        g, i = t // DIRECT, t % DIRECT
        top = jnp.minimum(req_s[i, LANE_TILE], 1) * TW
        left = req_s[i, LANE_DOM + g] * TW
        sent[g, i] = orbs[pl.ds(top, TW), pl.ds(left, TW)]

        @pl.when(target(i) != bas)
        def _():
            block_copy(g, i).start()

        @pl.when(target(i) == bas)
        def _():
            block_self(g, i).start()

    def fill(j, base, read):
        at = half_holder(y0, j)
        cols = pl.ds(pl.multiple_of(j * TW, TW), TW)
        for m in range(2):
            keep = rec_s[at, LANE_ON] * jnp.where(rec_s[at, LANE_ROW] == m, 1, 0)
            scale = keep.astype(jnp.float32)
            for p in range(2):
                part = read(at, p).astype(jnp.float32) * scale
                lhs[pl.ds(base + (2 * m + p) * TW, TW), cols] = part.astype(jnp.bfloat16)

    @pl.loop(0, HALF)
    def _(j):
        fill(j, 0, lambda at, p: ints[p, slot_of(at)])

    rec_doms = [dom_copy(0), dom_copy(1)]
    for copy in rec_doms:
        copy.wait()
    dom_local = pltpu.make_async_copy(domv, dom_s, load_sem.at[4])
    dom_local.start()
    dom_local.wait()

    @pl.loop(0, 8)
    def _(t):
        m, k = t // 4, t % 4
        n = jnp.clip(pair_ref[m, k] - 2 * bas + 2, 0, 5)
        side, row = n >> 1, n & 1
        match_s[t, 12] = side
        match_s[t, 13] = row
        for d in range(DOM):
            at, some = 0, 0
            for e in range(DOM):
                same = jnp.where(dom_s[side, 0, row * DOM + e] == dom_ref[m, d], 1, 0)
                at, some = at + same * e, some + same
            match_s[t, d] = jnp.minimum(at, DOM - 1)
            match_s[t, DOM + d] = some

    def whole(ref, sem):
        return pltpu.make_async_copy(ref, ref, sem)

    def part_copy(g):
        return pltpu.make_async_remote_copy(
            src_ref=other.at[g], dst_ref=other_in.at[g],
            send_sem=part_send.at[g], recv_sem=part_recv.at[g],
            device_id={"aux": partner}, device_id_type=MESH,
        )

    def halo_copy(g, way):
        return pltpu.make_async_remote_copy(
            src_ref=halo.at[1, g], dst_ref=halo.at[2 - 2 * way, g],
            send_sem=halo_send.at[g, way], recv_sem=halo_recv.at[g, way],
            device_id={"bas": after if way else before}, device_id_type=MESH,
        )

    def contract(into, base, g):
        into[g] = jnp.dot(lhs[base : base + ROWS, :], rhs[g], preferred_element_type=jnp.float32)

    def finish(g):
        part_copy(g).wait_recv()
        for m in range(2):
            for p in range(2):
                rows = pl.ds((2 * m + p) * TW, TW)
                total = own[g, rows, :] + other_in[g, rows, :]
                halo[1, g, m, :, p * TW : (p + 1) * TW] = total.astype(jnp.bfloat16)
        halo_copy(g, 0).start()
        halo_copy(g, 1).start()

    def passed(g):
        whole(rhs.at[g, pl.ds(DIRECT * TW, DIRECT * TW), :], pass_recv.at[g]).wait()

    for g in range(DOM):
        @pl.loop(0, DIRECT)
        def _(i):
            block_self(g, i).wait()
            pass_copy(g, i).start()

        if g == 4:
            ints_copy.wait_recv()

            @pl.loop(0, HALF)
            def _(j):
                fill(j, ROWS, lambda at, p: ints_in[j, p])

            for early in range(3):
                contract(other, ROWS, early)
                part_copy(early).start()
        if g >= 1:
            passed(g - 1)
            if g >= 4:
                contract(other, ROWS, g - 1)
                part_copy(g - 1).start()
            contract(own, 0, g - 1)
    last = DOM - 1
    for g in range(last - 1):
        finish(g)
    passed(last)
    contract(other, ROWS, last)
    part_copy(last).start()
    contract(own, 0, last)
    finish(last - 1)
    finish(last)
    for g in range(DOM):
        halo_copy(g, 0).wait_recv()
        halo_copy(g, 1).wait_recv()

    def tile_copy(r):
        owner = (y + r) % 4
        return pltpu.make_async_remote_copy(
            src_ref=tiles.at[pl.ds(2 * owner, 2)], dst_ref=tiles_in.at[r - 1],
            send_sem=tile_send.at[r - 1], recv_sem=tile_recv.at[r - 1],
            device_id={"aux": owner}, device_id_type=MESH,
        )

    def res_copy(r):
        return pltpu.make_async_remote_copy(
            src_ref=result.at[pl.ds(2 * y, 2)], dst_ref=result.at[pl.ds(2 * y, 2)],
            send_sem=res_send.at[r - 1], recv_sem=res_recv.at[r - 1],
            device_id={"aux": (y + r) % 4}, device_id_type=MESH,
        )

    for r in (2, 1, 3, 0):
        @pl.loop(0, 2)
        def _(s):
            t = 2 * ((y + r) % 4) + s
            side, row = match_s[t, 12], match_s[t, 13]
            total = jnp.zeros((TW, TW), jnp.float32)
            for d in range(DOM):
                there = halo[side, match_s[t, d], row]
                scale = match_s[t, DOM + d].astype(jnp.float32)
                here = halo[1, d, t // 4]
                part = lax.dot_general(
                    here, there, (((1,), (1,)), ((), ())), preferred_element_type=jnp.float32
                )
                total += part * scale
            tiles[t] = total

        if r:
            tile_copy(r).start()
    for r in range(1, 4):
        tile_copy(r).wait_recv()
    total = tiles[pl.ds(2 * y, 2)] + tiles_in[0] + tiles_in[1] + tiles_in[2]
    result[pl.ds(2 * y, 2)] = total.astype(jnp.bfloat16)
    for r in (2, 1, 3):
        res_copy(r).start()

    @pl.loop(0, DOM * DIRECT)
    def _(t):
        g, i = t // DIRECT, t % DIRECT

        @pl.when(target(i) != bas)
        def _():
            block_copy(g, i).wait_send()

    @pl.loop(0, DIRECT)
    def _(i):
        @pl.when(holder(y0, y1, i) != bas)
        def _():
            rec_copy(i).wait_send()

    for g in range(DOM):
        whole(rhs.at[g, pl.ds(0, DIRECT * TW), :], pass_send.at[g]).wait()
        part_copy(g).wait_send()
        halo_copy(g, 0).wait_send()
        halo_copy(g, 1).wait_send()
    ints_copy.wait_send()
    for r in range(1, 4):
        tile_copy(r).wait_send()
        res_copy(r).wait()
    out_ref[...] = result[...]


def on_device(integrals, orbitals, screen_list, screen_count, domains, pair_list):
    vmem, smem = pl.BlockSpec(memory_space=pltpu.VMEM), pl.BlockSpec(memory_space=pltpu.SMEM)
    hbm = pl.BlockSpec(memory_space=pl.ANY)
    dma, bf16, f32, i32 = pltpu.SemaphoreType.DMA, jnp.bfloat16, jnp.float32, jnp.int32
    out = pl.pallas_call(
        kernel,
        out_shape=jax.ShapeDtypeStruct((8, TW, TW), bf16),
        in_specs=[vmem, smem, smem, smem, hbm, hbm],
        out_specs=vmem,
        scratch_shapes=[
            pltpu.VMEM((2, 64, TW, TW), bf16),
            pltpu.VMEM(orbitals.shape, bf16),
            pltpu.VMEM((64, TW), i32),
            pltpu.SMEM((64, TW), i32),
            pltpu.VMEM((DIRECT, TW), i32),
            pltpu.SMEM((DIRECT, TW), i32),
            pltpu.VMEM((3, 8, TW), i32),
            pltpu.SMEM((3, 8, TW), i32),
            pltpu.SMEM((8, 16), i32),
            pltpu.VMEM((DOM, DIRECT, TW, TW), bf16),
            pltpu.VMEM((DOM, HALF * TW, TW), bf16),
            pltpu.VMEM((HALF, 2, TW, TW), bf16),
            pltpu.VMEM((HALF, 2, TW, TW), bf16),
            pltpu.VMEM((2 * ROWS, HALF * TW), bf16),
            pltpu.VMEM((DOM, ROWS, TW), f32),
            pltpu.VMEM((DOM, ROWS, TW), f32),
            pltpu.VMEM((DOM, ROWS, TW), f32),
            pltpu.VMEM((3, DOM, 2, TW, 2 * TW), bf16),
            pltpu.VMEM((8, TW, TW), f32),
            pltpu.VMEM((3, 2, TW, TW), f32),
            pltpu.VMEM((8, TW, TW), bf16),
            dma((5,)), dma((DIRECT,)), dma((DIRECT,)), dma((2,)), dma((2,)),
            dma((DOM, DIRECT)), dma((DOM, DIRECT)), dma((DOM,)), dma((DOM,)), dma((2,)),
            dma((DOM,)), dma((DOM,)), dma((DOM, 2)), dma((DOM, 2)), dma((3,)), dma((3,)), dma((3,)), dma((3,)),
        ],
        compiler_params=pltpu.CompilerParams(
            collective_id=0, has_side_effects=True, vmem_limit_bytes=52 * 2**20
        ),
    )(
        screen_list, screen_count, domains, pair_list,
        integrals.reshape(2, 64, TW, TW), orbitals,
    )
    return out.reshape(2, 4, TW, TW)


def solution(mesh):
    in_specs = (
        P("aux", "bas", None, None, None),
        P("bas", None),
        P("bas", None),
        P("bas"),
        P("bas", None),
        P("bas", None),
    )
    return jax.shard_map(
        on_device, mesh=mesh, in_specs=in_specs, out_specs=P("bas", None, None, None), check_vma=False
    )
```

time: 496 us -> 141 us (0.28)
  waiting for transfers between devices: 281 us -> 0 us
  Pallas kernels: 0 us -> 137 us
  blocking collectives: 111 us -> 0 us
  local copies, waits for them, and re-layouts: 52.7 us -> 3.4 us
  matrix products: 16.5 us -> 0 us
  starting transfers between devices: 15.7 us -> 0 us
  other arithmetic: 15.1 us -> 0 us
    all_to_all x1 -> x0, waiting for transfers between devices: 275 us -> none  [on_device(): lax.all_to_all(picked, 'bas', split_axis=0, concat_axis=0, tiled=True)]
    pallas_call x0 -> x1, Pallas kernels: none -> 137 us  [on_device(): pl.pallas_call(kernel, out_shape=jax.ShapeDtypeStruct((8, TW, TW), bf16),...]
    all_gather x2 -> x0, blocking collectives: 90.9 us -> none  [the longest x1 48.2 us: on_device(): lax.all_gather(screen_list, 'bas', axis=0, tiled=True)]
    gather x4 -> x0, local copies, waits for them, and re-layouts: 33.9 us -> none  [the longest x1 18.9 us: on_device(): blocked[jnp.maximum(local_tile, 0)[:, None], :, flat_records[:, 1:], :]]
    psum x1 -> x0, blocking collectives: 20 us -> none  [on_device(): summed = lax.psum(partial_value, 'aux')]
    dot_general x3 -> x0, matrix products: 16.5 us -> none  [the longest x1 11.9 us: on_device(): jnp.einsum('pmsab,msdbo->mapdo', integrals, fetched, preferred_element_ty...]
    reshape x4 -> x0, local copies, waits for them, and re-layouts: 11.5 us -> none  [the longest x1 7.62 us: on_device(): rim_half[partner_row]]
    select_n x5 -> x0, other arithmetic: 10.8 us -> none  [the longest x1 10.8 us: on_device(): jnp.where((local_tile >= 0)[:, None, None, None], picked, jnp.zeros((), p...]
  transfers between devices with their start and end apart: 5 -> 0, of which waited for: 3 -> 0; matrix products, arithmetic and copies ran while one was open for 0% -> 0% of each run, Pallas kernels for 0% -> 0%
where the time goes in v1:
time: 141 us
  Pallas kernels  137 us (97%)
  local copies, waits for them, and re-layouts  3.4 us (2%)
    pallas_call x1, Pallas kernels, on_device(): pl.pallas_call(kernel, out_shape=jax.ShapeDtypeStruct((8, TW, TW), bf16),...  137 us
    unnamed x9, local copies, waits for them, and re-layouts  3.4 us

profile of v1, /device:TPU:1, one launch (start us, length us, event | category | flops | bytes accessed | tf_op | source)
XLA Modules:
  0.0 140.7 jit_solution(5521924359932705981)
XLA Ops:
  0.0 0.0 copy-start
  0.0 0.7 copy-done
  0.7 0.0 copy-start.1
  0.7 0.7 copy-done.1
  1.4 0.0 copy-start.2
  1.4 0.7 copy-done.2
  2.0 0.0 copy-start.3
  2.0 0.7 copy-done.3
  2.7 137.3 %shard_map.64 = bf16[8,128,128]{2,1,0:T(8,128)(2,1)S(1)} custom-call(s32[2,32]{1,0:T(2,128)S(1)} %copy-done, s32[2]{0:T(128)S(1)} %copy-done.3, s32[2,6]{1,0:T(2,128)S(1)} %copy-done.1, s32[2,4]{1,0:T(2,128)S(1)} %copy-done.2, bf16[2,64,128,128]{3,2,1,0:T(8,128)(2,1)} %bitcast.3, bf16[256,10240]{1,0:T(8,128)(2,1)} %orbitals_ref.1), custom_call_target="tpu_custom_call" | custom-call | tf_op jit(solution)/shard_map/pallas_call | solution.py:369
  140.0 0.7 copy.8
Async XLA Ops:
  0.0 0.7 copy-start
  0.7 0.7 copy-start.1
  1.4 0.7 copy-start.2
  2.0 0.7 copy-start.3

commit v2 on v1

v2 whole, which is shorter than its diff:
```python
import functools

import jax
import jax.numpy as jnp
from jax import lax
from jax.experimental import pallas as pl
from jax.experimental.pallas import tpu as pltpu
from jax.sharding import PartitionSpec as P

MESH = pl.DeviceIdType.MESH
TW = 128
DOM = 6
FAR = 14
NEAR = 8
HALF = 2 * FAR
HELD = HALF + NEAR
ROWS = 4 * TW
LANE_TILE, LANE_DOM, LANE_SLOT, LANE_ROW, LANE_ON = 0, 1, 7, 8, 9


def kernel(
    lists_ref, count_ref, dom_ref, pair_ref, integrals_ref, orbitals_ref, out_ref,
    lists, count, dom, pair,
    ints, orbs, rec, rec_s, req, req_s, domv, dom_s, match_s,
    sent, rhs, ints_out, ints_in, lhs, own, other, other_in, halo, tiles, tiles_in, result,
    load_sem, rec_send, rec_recv, dom_send, dom_recv,
    block_send, block_recv, pass_send, pass_recv, ints_sem,
    part_send, part_recv, halo_send, halo_recv, tile_send, tile_recv, res_send, res_recv,
):
    y, bas = lax.axis_index("aux"), lax.axis_index("bas")
    x, z, c = lax.div(bas, 16), lax.rem(lax.div(bas, 2), 8), lax.rem(bas, 2)
    y0, y1 = lax.rem(y, 2), lax.div(y, 2)
    partner, mate = y + 1 - 2 * y0, 3 - y
    before, after = lax.rem(bas + 63, 64), lax.rem(bas + 1, 64)

    def place(px, pz, pc):
        return lax.rem(px, 4) * 16 + lax.rem(pz, 8) * 2 + pc

    def offset(parity, i):
        dz = lax.rem(i, 7) + 1
        return 2 * lax.div(i, 7) + lax.rem(dz + parity, 2), dz

    out_parity = lax.rem(c + y0, 2)
    out_core = lax.rem(y0 + y1 + c, 2)

    def target(i):
        dx, dz = offset(out_parity, i)
        return place(x + 4 - dx, z + 8 - dz, out_core)

    def holder(plane0, plane1, i):
        dx, dz = offset(lax.rem(c + plane1, 2), i)
        return place(x + dx, z + dz, lax.rem(plane0 + plane1 + c, 2))

    def half_holder(plane0, j):
        q = lax.div(j, FAR)
        return holder(lax.rem(plane0 + q, 2), lax.rem(y1 + q, 2), lax.rem(j, FAR))

    def near_target(v):
        return place(x + 4 - lax.div(v, 2), z, lax.rem(c + v, 2))

    def near_holder(v):
        return place(x + lax.div(v, 2), z, lax.rem(c + v, 2))

    small = [
        pltpu.make_async_copy(a, b, load_sem.at[5 + i])
        for i, (a, b) in enumerate(
            [(lists_ref, lists), (count_ref, count), (dom_ref, dom), (pair_ref, pair)]
        )
    ]
    load_ints = pltpu.make_async_copy(integrals_ref, ints, load_sem.at[0])
    load_orbs = pltpu.make_async_copy(orbitals_ref, orbs, load_sem.at[1])
    for copy in small:
        copy.start()
    load_ints.start()
    load_orbs.start()

    barrier = pltpu.get_barrier_semaphore()

    def greet(device):
        pl.semaphore_signal(barrier, inc=1, device_id=device, device_id_type=MESH)

    @pl.loop(0, FAR)
    def _(i):
        greet({"bas": target(i)})
        greet({"bas": holder(y0, y1, i)})

    @pl.loop(1, NEAR)
    def _(v):
        greet({"bas": near_target(v)})

    for r in range(1, 4):
        greet({"aux": lax.rem(y + r, 4)})
    greet({"bas": before})
    greet({"bas": after})

    for copy in small:
        copy.wait()

    holder_ids = lax.broadcasted_iota(jnp.int32, (64, 32), 0)
    slot_ids = lax.broadcasted_iota(jnp.int32, (64, 32), 1)
    lanes = lax.broadcasted_iota(jnp.int32, (64, TW), 1)
    table = jnp.zeros((64, TW), jnp.int32)
    for m in range(2):
        row = lists[m : m + 1, :]
        hit = (row >> 1) == holder_ids
        found = jnp.sum(jnp.where(hit, 1, 0), axis=1, keepdims=True)
        tile = jnp.sum(jnp.where(hit, row & 1, 0), axis=1, keepdims=True)
        slot = jnp.sum(jnp.where(hit, slot_ids, 0), axis=1, keepdims=True)
        on = found * jnp.where(slot < count[m], 1, 0)
        table += jnp.where(lanes == LANE_TILE, tile, 0)
        table += jnp.where(lanes == LANE_SLOT, slot + found * (32 * m), 0)
        table += jnp.where(lanes == LANE_ROW, found * m, 0)
        table += jnp.where(lanes == LANE_ON, on, 0)
        for d in range(DOM):
            table += jnp.where(lanes == LANE_DOM + d, found * dom[m, d], 0)
    rec[...] = jnp.clip(table, 0, 79)
    lane = lax.broadcasted_iota(jnp.int32, (8, TW), 1)
    mine = jnp.zeros((8, TW), jnp.int32)
    for m in range(2):
        for d in range(DOM):
            mine += jnp.where(lane == m * DOM + d, dom[m, d], 0)
    domv[1] = mine
    rec_local = pltpu.make_async_copy(rec, rec_s, load_sem.at[2])
    rec_local.start()

    pl.semaphore_wait(barrier, 2 * FAR + NEAR - 1 + 5)

    def rec_copy(i, device):
        return pltpu.make_async_remote_copy(
            src_ref=rec.at[pl.ds(device, 1), :], dst_ref=req.at[pl.ds(i, 1), :],
            send_sem=rec_send.at[i], recv_sem=rec_recv.at[i],
            device_id={"bas": device}, device_id_type=MESH,
        )

    def rec_far(i):
        return rec_copy(i, holder(y0, y1, i))

    def rec_near(v):
        return rec_copy(FAR + v, near_holder(v))

    rec_self = pltpu.make_async_copy(rec.at[pl.ds(bas, 1), :], req.at[pl.ds(FAR, 1), :], rec_recv.at[FAR])

    @pl.loop(0, FAR)
    def _(i):
        rec_far(i).start()

    @pl.loop(1, NEAR)
    def _(v):
        rec_near(v).start()

    rec_self.start()

    def dom_copy(way):
        return pltpu.make_async_remote_copy(
            src_ref=domv.at[1], dst_ref=domv.at[2 - 2 * way],
            send_sem=dom_send.at[way], recv_sem=dom_recv.at[way],
            device_id={"bas": after if way else before}, device_id_type=MESH,
        )

    dom_copy(0).start()
    dom_copy(1).start()

    def slot_of(at):
        return jnp.minimum(rec_s[at, LANE_SLOT], 63)

    rec_local.wait()
    load_ints.wait()

    @pl.loop(0, HALF)
    def _(j):
        slot = slot_of(half_holder(lax.rem(y0 + 1, 2), j))
        for p in range(2):
            ints_out[j, p] = ints[p, slot]

    ints_copy = pltpu.make_async_remote_copy(
        src_ref=ints_out, dst_ref=ints_in, send_sem=ints_sem.at[0], recv_sem=ints_sem.at[1],
        device_id={"aux": partner}, device_id_type=MESH,
    )
    ints_copy.start()

    rec_self.wait()

    @pl.loop(0, FAR)
    def _(i):
        rec_far(i).wait_recv()

    @pl.loop(1, NEAR)
    def _(v):
        rec_near(v).wait_recv()

    req_local = pltpu.make_async_copy(req, req_s, load_sem.at[3])
    req_local.start()
    req_local.wait()
    load_orbs.wait()

    def rows_of(i):
        return pl.ds(pl.multiple_of(i * TW, TW), TW)

    def block_copy(g, i):
        return pltpu.make_async_remote_copy(
            src_ref=sent.at[g, i], dst_ref=rhs.at[g, rows_of(i), :],
            send_sem=block_send.at[g, i], recv_sem=block_recv.at[g, i],
            device_id={"bas": target(i)}, device_id_type=MESH,
        )

    def near_copy(g, v):
        return pltpu.make_async_remote_copy(
            src_ref=sent.at[g, FAR + v], dst_ref=rhs.at[g, rows_of(HALF + v), :],
            send_sem=block_send.at[g, FAR + v], recv_sem=block_recv.at[g, FAR + v],
            device_id={"bas": near_target(v)}, device_id_type=MESH,
        )

    def self_copy(g):
        return pltpu.make_async_copy(
            sent.at[g, FAR], rhs.at[g, pl.ds(HALF * TW, TW), :], block_recv.at[g, FAR]
        )

    def pass_copy(g, i):
        return pltpu.make_async_remote_copy(
            src_ref=rhs.at[g, rows_of(i), :], dst_ref=rhs.at[g, rows_of(FAR + i), :],
            send_sem=pass_send.at[g], recv_sem=pass_recv.at[g],
            device_id={"aux": mate}, device_id_type=MESH,
        )

    def pick(g, i):
        top = jnp.minimum(req_s[i, LANE_TILE], 1) * TW
        left = req_s[i, LANE_DOM + g] * TW
        sent[g, i] = orbs[pl.ds(top, TW), pl.ds(left, TW)]

    @pl.loop(0, DOM)
    def _(g):
        @pl.loop(0, FAR)
        def _(i):
            pick(g, i)
            block_copy(g, i).start()

        @pl.loop(1, NEAR)
        def _(v):
            pick(g, FAR + v)
            near_copy(g, v).start()

        pick(g, FAR)
        self_copy(g).start()

    def fill(j, at, base, read):
        cols = pl.ds(pl.multiple_of(j * TW, TW), TW)
        for m in range(2):
            keep = rec_s[at, LANE_ON] * jnp.where(rec_s[at, LANE_ROW] == m, 1, 0)
            scale = keep.astype(jnp.float32)
            for p in range(2):
                part = read(at, p).astype(jnp.float32) * scale
                lhs[pl.ds(base + (2 * m + p) * TW, TW), cols] = part.astype(jnp.bfloat16)

    def mine_at(at, p):
        return ints[p, slot_of(at)]

    @pl.loop(0, HALF)
    def _(j):
        fill(j, half_holder(y0, j), 0, mine_at)

    @pl.loop(0, NEAR)
    def _(v):
        fill(HALF + v, near_holder(v), 0, mine_at)

    rec_doms = [dom_copy(0), dom_copy(1)]
    for copy in rec_doms:
        copy.wait()
    dom_local = pltpu.make_async_copy(domv, dom_s, load_sem.at[4])
    dom_local.start()
    dom_local.wait()

    @pl.loop(0, 8)
    def _(t):
        m, k = lax.div(t, 4), lax.rem(t, 4)
        n = jnp.clip(pair[m, k] - 2 * bas + 2, 0, 5)
        side, row = n >> 1, n & 1
        match_s[t, 12] = side
        match_s[t, 13] = row
        for d in range(DOM):
            at, some = 0, 0
            for e in range(DOM):
                same = jnp.where(dom_s[side, 0, row * DOM + e] == dom[m, d], 1, 0)
                at, some = at + same * e, some + same
            match_s[t, d] = jnp.minimum(at, DOM - 1)
            match_s[t, DOM + d] = some

    def whole(ref, sem):
        return pltpu.make_async_copy(ref, ref, sem)

    def part_copy(g, m):
        return pltpu.make_async_remote_copy(
            src_ref=other.at[g, m], dst_ref=other_in.at[g, m],
            send_sem=part_send.at[g, m], recv_sem=part_recv.at[g, m],
            device_id={"aux": partner}, device_id_type=MESH,
        )

    def halo_copy(g, m, way):
        return pltpu.make_async_remote_copy(
            src_ref=halo.at[1, g, m], dst_ref=halo.at[2 - 2 * way, g, m],
            send_sem=halo_send.at[g, m, way], recv_sem=halo_recv.at[g, m, way],
            device_id={"bas": after if way else before}, device_id_type=MESH,
        )

    def contract_own(g):
        for m in range(2):
            own[g, m] = jnp.dot(
                lhs[2 * m * TW : 2 * (m + 1) * TW, :], rhs[g], preferred_element_type=jnp.float32
            )

    def contract_other(g):
        for m in range(2):
            rows = pl.ds(ROWS + 2 * m * TW, 2 * TW)
            other[g, m] = jnp.dot(
                lhs[rows, : HALF * TW], rhs[g, : HALF * TW, :], preferred_element_type=jnp.float32
            )
            part_copy(g, m).start()

    def finish(g):
        for m in range(2):
            part_copy(g, m).wait_recv()
            for p in range(2):
                rows = pl.ds(p * TW, TW)
                total = own[g, m, rows, :] + other_in[g, m, rows, :]
                halo[1, g, m, :, p * TW : (p + 1) * TW] = total.astype(jnp.bfloat16)
            halo_copy(g, m, 0).start()
            halo_copy(g, m, 1).start()

    def arrived(g):
        self_copy(g).wait()

        @pl.loop(1, NEAR)
        def _(v):
            near_copy(g, v).wait_recv()

        whole(rhs.at[g, pl.ds(FAR * TW, FAR * TW), :], pass_recv.at[g]).wait()

    def hand_on(g, low, high):
        @pl.loop(low, high)
        def _(i):
            block_copy(g, i).wait_recv()
            pass_copy(g, i).start()

    last = DOM - 1
    for g in range(DOM):
        hand_on(g, 0, FAR // 2)
        if g == 3:
            ints_copy.wait_recv()

            @pl.loop(0, HALF)
            def _(j):
                fill(j, half_holder(y0, j), ROWS, lambda at, p: ints_in[j, p])

            contract_other(0)
            contract_other(1)
        if g >= 1:
            arrived(g - 1)
            if g >= 3:
                contract_other(g - 1)
            contract_own(g - 1)
        hand_on(g, FAR // 2, FAR)
        if g == last:
            for early in range(last - 2):
                finish(early)
    arrived(last)
    contract_other(last)
    finish(last - 2)
    contract_own(last)
    finish(last - 1)
    finish(last)
    for g in range(DOM):
        for m in range(2):
            halo_copy(g, m, 0).wait_recv()
            halo_copy(g, m, 1).wait_recv()

    def tile_copy(r):
        owner = lax.rem(y + r, 4)
        return pltpu.make_async_remote_copy(
            src_ref=tiles.at[pl.ds(2 * owner, 2)], dst_ref=tiles_in.at[r - 1],
            send_sem=tile_send.at[r - 1], recv_sem=tile_recv.at[r - 1],
            device_id={"aux": owner}, device_id_type=MESH,
        )

    def res_copy(r):
        return pltpu.make_async_remote_copy(
            src_ref=result.at[pl.ds(2 * y, 2)], dst_ref=result.at[pl.ds(2 * y, 2)],
            send_sem=res_send.at[r - 1], recv_sem=res_recv.at[r - 1],
            device_id={"aux": lax.rem(y + r, 4)}, device_id_type=MESH,
        )

    for r in (2, 1, 3, 0):
        @pl.loop(0, 2)
        def _(s):
            t = 2 * lax.rem(y + r, 4) + s
            side, row = match_s[t, 12], match_s[t, 13]
            total = jnp.zeros((TW, TW), jnp.float32)
            for d in range(DOM):
                there = halo[side, match_s[t, d], row]
                scale = match_s[t, DOM + d].astype(jnp.float32)
                here = halo[1, d, lax.div(t, 4)]
                part = lax.dot_general(
                    here, there, (((1,), (1,)), ((), ())), preferred_element_type=jnp.float32
                )
                total += part * scale
            tiles[t] = total

        if r:
            tile_copy(r).start()
    for r in range(1, 4):
        tile_copy(r).wait_recv()
    total = tiles[pl.ds(2 * y, 2)] + tiles_in[0] + tiles_in[1] + tiles_in[2]
    result[pl.ds(2 * y, 2)] = total.astype(jnp.bfloat16)
    for r in (2, 1, 3):
        res_copy(r).start()

    @pl.loop(0, DOM)
    def _(g):
        @pl.loop(0, FAR)
        def _(i):
            block_copy(g, i).wait_send()

        @pl.loop(1, NEAR)
        def _(v):
            near_copy(g, v).wait_send()

        whole(rhs.at[g, pl.ds(0, FAR * TW), :], pass_send.at[g]).wait()
        for m in range(2):
            part_copy(g, m).wait_send()
            halo_copy(g, m, 0).wait_send()
            halo_copy(g, m, 1).wait_send()

    @pl.loop(0, FAR)
    def _(i):
        rec_far(i).wait_send()

    @pl.loop(1, NEAR)
    def _(v):
        rec_near(v).wait_send()

    ints_copy.wait_send()
    for r in range(1, 4):
        tile_copy(r).wait_send()
        res_copy(r).wait()
    out_ref[...] = result[...]


def on_device(integrals, orbitals, screen_list, screen_count, domains, pair_list):
    vmem = pl.BlockSpec(memory_space=pltpu.VMEM)
    hbm = pl.BlockSpec(memory_space=pltpu.HBM)
    dma, bf16, f32, i32 = pltpu.SemaphoreType.DMA, jnp.bfloat16, jnp.float32, jnp.int32
    out = pl.pallas_call(
        kernel,
        out_shape=jax.ShapeDtypeStruct((8, TW, TW), bf16),
        in_specs=[hbm] * 6,
        out_specs=vmem,
        scratch_shapes=[
            pltpu.VMEM(screen_list.shape, i32),
            pltpu.SMEM(screen_count.shape, i32),
            pltpu.SMEM(domains.shape, i32),
            pltpu.SMEM(pair_list.shape, i32),
            pltpu.VMEM((2, 64, TW, TW), bf16),
            pltpu.VMEM(orbitals.shape, bf16),
            pltpu.VMEM((64, TW), i32),
            pltpu.SMEM((64, TW), i32),
            pltpu.VMEM((24, TW), i32),
            pltpu.SMEM((24, TW), i32),
            pltpu.VMEM((3, 8, TW), i32),
            pltpu.SMEM((3, 8, TW), i32),
            pltpu.SMEM((8, 16), i32),
            pltpu.VMEM((DOM, FAR + NEAR, TW, TW), bf16),
            pltpu.VMEM((DOM, HELD * TW, TW), bf16),
            pltpu.VMEM((HALF, 2, TW, TW), bf16),
            pltpu.VMEM((HALF, 2, TW, TW), bf16),
            pltpu.VMEM((2 * ROWS, HELD * TW), bf16),
            pltpu.VMEM((DOM, 2, 2 * TW, TW), f32),
            pltpu.VMEM((DOM, 2, 2 * TW, TW), f32),
            pltpu.VMEM((DOM, 2, 2 * TW, TW), f32),
            pltpu.VMEM((3, DOM, 2, TW, 2 * TW), bf16),
            pltpu.VMEM((8, TW, TW), f32),
            pltpu.VMEM((3, 2, TW, TW), f32),
            pltpu.VMEM((8, TW, TW), bf16),
            dma((9,)), dma((FAR + NEAR,)), dma((FAR + NEAR,)), dma((2,)), dma((2,)),
            dma((DOM, FAR + NEAR)), dma((DOM, FAR + NEAR)), dma((DOM,)), dma((DOM,)), dma((2,)),
            dma((DOM, 2)), dma((DOM, 2)), dma((DOM, 2, 2)), dma((DOM, 2, 2)),
            dma((3,)), dma((3,)), dma((3,)), dma((3,)),
        ],
        compiler_params=pltpu.CompilerParams(
            collective_id=0, has_side_effects=True, vmem_limit_bytes=64 * 2**20 - 2**16
        ),
    )(
        screen_list, screen_count, domains, pair_list,
        integrals.reshape(2, 64, TW, TW), orbitals,
    )
    return out.reshape(2, 4, TW, TW)


def solution(mesh):
    in_specs = (
        P("aux", "bas", None, None, None),
        P("bas", None),
        P("bas", None),
        P("bas"),
        P("bas", None),
        P("bas", None),
    )
    return jax.shard_map(
        on_device, mesh=mesh, in_specs=in_specs, out_specs=P("bas", None, None, None), check_vma=False
    )
```

time: 141 us -> 122 us (0.87)
  Pallas kernels: 137 us -> 120 us
  local copies, waits for them, and re-layouts: 3.4 us -> 1.67 us
    pallas_call x1, Pallas kernels: 137 us -> 120 us  [on_device(): pl.pallas_call(kernel, out_shape=jax.ShapeDtypeStruct((8, TW, TW), bf16),...]
    unnamed x9 -> x1, local copies, waits for them, and re-layouts: 3.4 us -> 1.67 us
where the time goes in v2:
time: 122 us
  Pallas kernels  120 us (98%)
  local copies, waits for them, and re-layouts  1.67 us (1%)
    pallas_call x1, Pallas kernels, on_device(): pl.pallas_call(kernel, out_shape=jax.ShapeDtypeStruct((8, TW, TW), bf16),...  120 us

profile of v2, /device:TPU:1, one launch (start us, length us, event | category | flops | bytes accessed | tf_op | source)
XLA Modules:
  0.0 121.7 jit_solution(5907558100668105719)
XLA Ops:
  0.0 120.0 %shard_map.64 = bf16[8,128,128]{2,1,0:T(8,128)(2,1)} custom-call(s32[2,32]{1,0:T(2,128)} %lists_ref.1, s32[2]{0:T(128)} %count_ref.1, s32[2,6]{1,0:T(2,128)} %dom_ref.1, s32[2,4]{1,0:T(2,128)} %pair_ref.1, bf16[2,64,128,128]{3,2,1,0:T(8,128)(2,1)} %bitcast.2, bf16[256,10240]{1,0:T(8,128)(2,1)} %orbitals_ref.1), custom_call_target="tpu_custom_call" | custom-call | tf_op jit(solution)/shard_map/pallas_call | solution.py:450
  120.1 1.7 %copy.8 = bf16[2,4,128,128]{3,2,1,0:T(8,128)(2,1)} copy(bf16[2,4,128,128]{3,2,1,0:T(8,128)(2,1)} %bitcast.3) | data formatting | bytes 524288

commit v3 on v2

--- a/solution.py
+++ b/solution.py
@@ -14,7 +14,10 @@
 NEAR = 8
 HALF = 2 * FAR
 HELD = HALF + NEAR
+AHEAD = 2
 ROWS = 4 * TW
+LAST = DOM - 1
+SIDE, ROW, BACK, SOME_BACK, BOTH = 12, 13, 14, 15, 16
 LANE_TILE, LANE_DOM, LANE_SLOT, LANE_ROW, LANE_ON = 0, 1, 7, 8, 9
 
 
@@ -22,7 +25,7 @@
     lists_ref, count_ref, dom_ref, pair_ref, integrals_ref, orbitals_ref, out_ref,
     lists, count, dom, pair,
     ints, orbs, rec, rec_s, req, req_s, domv, dom_s, match_s,
-    sent, rhs, ints_out, ints_in, lhs, own, other, other_in, halo, tiles, tiles_in, result,
+    sent, rhs, ints_out, ints_in, lhs, own, other, other_in, halo, final, tiles, tiles_in, result,
     load_sem, rec_send, rec_recv, dom_send, dom_recv,
     block_send, block_recv, pass_send, pass_recv, ints_sem,
     part_send, part_recv, halo_send, halo_recv, tile_send, tile_recv, res_send, res_recv,
@@ -37,7 +40,8 @@
         return lax.rem(px, 4) * 16 + lax.rem(pz, 8) * 2 + pc
 
     def offset(parity, i):
-        dz = lax.rem(i, 7) + 1
+        v = lax.rem(i, 7)
+        dz = 4 + lax.div(v + 1, 2) * (1 - 2 * lax.rem(v, 2))
         return 2 * lax.div(i, 7) + lax.rem(dz + parity, 2), dz
 
     out_parity = lax.rem(c + y0, 2)
@@ -227,13 +231,11 @@
         left = req_s[i, LANE_DOM + g] * TW
         sent[g, i] = orbs[pl.ds(top, TW), pl.ds(left, TW)]
 
-    @pl.loop(0, DOM)
-    def _(g):
-        @pl.loop(0, FAR)
-        def _(i):
-            pick(g, i)
-            block_copy(g, i).start()
-
+    def send_far(g, i):
+        pick(g, i)
+        block_copy(g, i).start()
+
+    def send_near(g):
         @pl.loop(1, NEAR)
         def _(v):
             pick(g, FAR + v)
@@ -241,6 +243,13 @@
 
         pick(g, FAR)
         self_copy(g).start()
+
+    for g in range(AHEAD):
+        @pl.loop(0, FAR)
+        def _(i):
+            send_far(g, i)
+
+        send_near(g)
 
     def fill(j, at, base, read):
         cols = pl.ds(pl.multiple_of(j * TW, TW), TW)
@@ -254,35 +263,44 @@
     def mine_at(at, p):
         return ints[p, slot_of(at)]
 
-    @pl.loop(0, HALF)
-    def _(j):
-        fill(j, half_holder(y0, j), 0, mine_at)
-
-    @pl.loop(0, NEAR)
-    def _(v):
-        fill(HALF + v, near_holder(v), 0, mine_at)
-
-    rec_doms = [dom_copy(0), dom_copy(1)]
-    for copy in rec_doms:
-        copy.wait()
-    dom_local = pltpu.make_async_copy(domv, dom_s, load_sem.at[4])
-    dom_local.start()
-    dom_local.wait()
-
-    @pl.loop(0, 8)
-    def _(t):
-        m, k = lax.div(t, 4), lax.rem(t, 4)
-        n = jnp.clip(pair[m, k] - 2 * bas + 2, 0, 5)
-        side, row = n >> 1, n & 1
-        match_s[t, 12] = side
-        match_s[t, 13] = row
-        for d in range(DOM):
-            at, some = 0, 0
-            for e in range(DOM):
-                same = jnp.where(dom_s[side, 0, row * DOM + e] == dom[m, d], 1, 0)
-                at, some = at + same * e, some + same
-            match_s[t, d] = jnp.minimum(at, DOM - 1)
-            match_s[t, DOM + d] = some
+    def fill_own():
+        @pl.loop(0, HALF)
+        def _(j):
+            fill(j, half_holder(y0, j), 0, mine_at)
+
+        @pl.loop(0, NEAR)
+        def _(v):
+            fill(HALF + v, near_holder(v), 0, mine_at)
+
+    def match():
+        for way in range(2):
+            dom_copy(way).wait()
+        dom_local = pltpu.make_async_copy(domv, dom_s, load_sem.at[4])
+        dom_local.start()
+        dom_local.wait()
+
+        @pl.loop(0, 8)
+        def _(t):
+            m, k = lax.div(t, 4), lax.rem(t, 4)
+            n = jnp.clip(pair[m, k] - 2 * bas + 2, 0, 5)
+            side, row = n >> 1, n & 1
+            match_s[t, SIDE] = side
+            match_s[t, ROW] = row
+            back, some_back = 0, 0
+            for d in range(DOM):
+                at, some = 0, 0
+                for e in range(LAST):
+                    same = jnp.where(dom_s[side, 0, row * DOM + e] == dom[m, d], 1, 0)
+                    at, some = at + same * e, some + same
+                match_s[t, d] = jnp.minimum(at, LAST - 1)
+                match_s[t, DOM + d] = some
+                same = jnp.where(dom_s[side, 0, row * DOM + LAST] == dom[m, d], 1, 0)
+                if d < LAST:
+                    back, some_back = back + same * d, some_back + same
+                else:
+                    match_s[t, BOTH] = same
+            match_s[t, BACK] = jnp.minimum(back, LAST - 1)
+            match_s[t, SOME_BACK] = some_back
 
     def whole(ref, sem):
         return pltpu.make_async_copy(ref, ref, sem)
@@ -296,7 +314,8 @@
 
     def halo_copy(g, m, way):
         return pltpu.make_async_remote_copy(
-            src_ref=halo.at[1, g, m], dst_ref=halo.at[2 - 2 * way, g, m],
+            src_ref=halo.at[1, g, m] if g < LAST else final.at[1, m],
+            dst_ref=halo.at[2 - 2 * way, g, m] if g < LAST else final.at[2 - 2 * way, m],
             send_sem=halo_send.at[g, m, way], recv_sem=halo_recv.at[g, m, way],
             device_id={"bas": after if way else before}, device_id_type=MESH,
         )
@@ -321,7 +340,10 @@
             for p in range(2):
                 rows = pl.ds(p * TW, TW)
                 total = own[g, m, rows, :] + other_in[g, m, rows, :]
-                halo[1, g, m, :, p * TW : (p + 1) * TW] = total.astype(jnp.bfloat16)
+                if g < LAST:
+                    halo[1, g, m, :, p * TW : (p + 1) * TW] = total.astype(jnp.bfloat16)
+                else:
+                    final[1, m, :, p * TW : (p + 1) * TW] = total.astype(jnp.bfloat16)
             halo_copy(g, m, 0).start()
             halo_copy(g, m, 1).start()
 
@@ -337,12 +359,15 @@
     def hand_on(g, low, high):
         @pl.loop(low, high)
         def _(i):
+            if g + AHEAD < DOM:
+                send_far(g + AHEAD, i)
             block_copy(g, i).wait_recv()
             pass_copy(g, i).start()
 
-    last = DOM - 1
     for g in range(DOM):
         hand_on(g, 0, FAR // 2)
+        if g == 0:
+            fill_own()
         if g == 3:
             ints_copy.wait_recv()
 
@@ -358,19 +383,58 @@
                 contract_other(g - 1)
             contract_own(g - 1)
         hand_on(g, FAR // 2, FAR)
-        if g == last:
-            for early in range(last - 2):
-                finish(early)
-    arrived(last)
-    contract_other(last)
-    finish(last - 2)
-    contract_own(last)
-    finish(last - 1)
-    finish(last)
-    for g in range(DOM):
+        if g + AHEAD < DOM:
+            send_near(g + AHEAD)
+        if g == 1:
+            match()
+    def columns(base, m, low, high):
+        return jnp.dot(
+            lhs[base + 2 * m * TW : base + 2 * (m + 1) * TW, low * TW : high * TW],
+            rhs[LAST, low * TW : high * TW, :], preferred_element_type=jnp.float32,
+        )
+
+    for m in range(2):
+        other[LAST, m] = columns(ROWS, m, 0, FAR)
+    for g in range(LAST - 1):
+        finish(g)
+    for m in range(2):
+        own[LAST, m] = columns(0, m, 0, FAR)
+    arrived(LAST)
+    for m in range(2):
+        other[LAST, m] += columns(ROWS, m, FAR, HALF)
+        part_copy(LAST, m).start()
+    for m in range(2):
+        own[LAST, m] += columns(0, m, FAR, HELD)
+    finish(LAST - 1)
+
+    def dot(here, there):
+        return lax.dot_general(here, there, (((1,), (1,)), ((), ())), preferred_element_type=jnp.float32)
+
+    def flag(t, column):
+        return match_s[t, column].astype(jnp.float32)
+
+    def wait_halo(g):
         for m in range(2):
             halo_copy(g, m, 0).wait_recv()
             halo_copy(g, m, 1).wait_recv()
+
+    def pairs(t, domains):
+        total = jnp.zeros((TW, TW), jnp.float32)
+        for d in domains:
+            here = halo[1, d, lax.div(t, 4)] if d < LAST else final[1, lax.div(t, 4)]
+            there = halo[match_s[t, SIDE], match_s[t, d], match_s[t, ROW]]
+            total += dot(here, there) * flag(t, DOM + d)
+        return total
+
+    finish(LAST)
+    for g in range(LAST):
+        wait_halo(g)
+
+    @pl.loop(0, 8)
+    def _(t):
+        tiles[t] = pairs(t, range(DOM))
+
+    wait_halo(LAST)
 
     def tile_copy(r):
         owner = lax.rem(y + r, 4)
@@ -388,21 +452,12 @@
         )
 
     for r in (2, 1, 3, 0):
-        @pl.loop(0, 2)
-        def _(s):
+        for s in range(2):
             t = 2 * lax.rem(y + r, 4) + s
-            side, row = match_s[t, 12], match_s[t, 13]
-            total = jnp.zeros((TW, TW), jnp.float32)
-            for d in range(DOM):
-                there = halo[side, match_s[t, d], row]
-                scale = match_s[t, DOM + d].astype(jnp.float32)
-                here = halo[1, d, lax.div(t, 4)]
-                part = lax.dot_general(
-                    here, there, (((1,), (1,)), ((), ())), preferred_element_type=jnp.float32
-                )
-                total += part * scale
-            tiles[t] = total
-
+            m = lax.div(t, 4)
+            here = halo[1, match_s[t, BACK], m].astype(jnp.float32) * flag(t, SOME_BACK)
+            here += final[1, m].astype(jnp.float32) * flag(t, BOTH)
+            tiles[t] += dot(here.astype(jnp.bfloat16), final[match_s[t, SIDE], match_s[t, ROW]])
         if r:
             tile_copy(r).start()
     for r in range(1, 4):
@@ -425,6 +480,9 @@
         whole(rhs.at[g, pl.ds(0, FAR * TW), :], pass_send.at[g]).wait()
         for m in range(2):
             part_copy(g, m).wait_send()
+
+    for g in range(DOM):
+        for m in range(2):
             halo_copy(g, m, 0).wait_send()
             halo_copy(g, m, 1).wait_send()
 
@@ -465,7 +523,7 @@
             pltpu.SMEM((24, TW), i32),
             pltpu.VMEM((3, 8, TW), i32),
             pltpu.SMEM((3, 8, TW), i32),
-            pltpu.SMEM((8, 16), i32),
+            pltpu.SMEM((8, 24), i32),
             pltpu.VMEM((DOM, FAR + NEAR, TW, TW), bf16),
             pltpu.VMEM((DOM, HELD * TW, TW), bf16),
             pltpu.VMEM((HALF, 2, TW, TW), bf16),
@@ -474,7 +532,8 @@
             pltpu.VMEM((DOM, 2, 2 * TW, TW), f32),
             pltpu.VMEM((DOM, 2, 2 * TW, TW), f32),
             pltpu.VMEM((DOM, 2, 2 * TW, TW), f32),
-            pltpu.VMEM((3, DOM, 2, TW, 2 * TW), bf16),
+            pltpu.VMEM((3, LAST, 2, TW, 2 * TW), bf16),
+            pltpu.VMEM((3, 2, TW, 2 * TW), bf16),
             pltpu.VMEM((8, TW, TW), f32),
             pltpu.VMEM((3, 2, TW, TW), f32),
             pltpu.VMEM((8, TW, TW), bf16),

time: 122 us -> 121 us (level)
  no operation moved by 1% of the time
where the time goes in v3:
time: 121 us
  Pallas kernels  119 us (98%)
  local copies, waits for them, and re-layouts  1.67 us (1%)
    pallas_call x1, Pallas kernels, on_device(): pl.pallas_call(kernel, out_shape=jax.ShapeDtypeStruct((8, TW, TW), bf16),...  119 us

profile of v3, /device:TPU:1, one launch (start us, length us, event | category | flops | bytes accessed | tf_op | source)
XLA Modules:
  0.0 120.8 jit_solution(17409824567070849727)
XLA Ops:
  0.0 119.1 %shard_map.64 = bf16[8,128,128]{2,1,0:T(8,128)(2,1)} custom-call(s32[2,32]{1,0:T(2,128)} %lists_ref.1, s32[2]{0:T(128)} %count_ref.1, s32[2,6]{1,0:T(2,128)} %dom_ref.1, s32[2,4]{1,0:T(2,128)} %pair_ref.1, bf16[2,64,128,128]{3,2,1,0:T(8,128)(2,1)} %bitcast.2, bf16[256,10240]{1,0:T(8,128)(2,1)} %orbitals_ref.1), custom_call_target="tpu_custom_call" | custom-call | tf_op jit(solution)/shard_map/pallas_call | solution.py:508
  119.1 1.7 %copy.8 = bf16[2,4,128,128]{3,2,1,0:T(8,128)(2,1)} copy(bf16[2,4,128,128]{3,2,1,0:T(8,128)(2,1)} %bitcast.3) | data formatting | bytes 524288

commit v4 on v3

--- a/solution.py
+++ b/solution.py
@@ -182,19 +182,12 @@
     )
     ints_copy.start()
 
-    rec_self.wait()
-
-    @pl.loop(0, FAR)
-    def _(i):
-        rec_far(i).wait_recv()
-
-    @pl.loop(1, NEAR)
-    def _(v):
-        rec_near(v).wait_recv()
-
-    req_local = pltpu.make_async_copy(req, req_s, load_sem.at[3])
-    req_local.start()
-    req_local.wait()
+    def to_scalars(low, high):
+        rows = pl.ds(low, high - low)
+        copy = pltpu.make_async_copy(req.at[rows, :], req_s.at[rows, :], load_sem.at[3])
+        copy.start()
+        copy.wait()
+
     load_orbs.wait()
 
     def rows_of(i):
@@ -245,9 +238,24 @@
         self_copy(g).start()
 
     for g in range(AHEAD):
-        @pl.loop(0, FAR)
-        def _(i):
-            send_far(g, i)
+        for low, high in ((0, 8), (8, FAR)):
+            if g == 0:
+                @pl.loop(low, high)
+                def _(i):
+                    rec_far(i).wait_recv()
+
+                if low:
+                    rec_self.wait()
+
+                    @pl.loop(1, NEAR)
+                    def _(v):
+                        rec_near(v).wait_recv()
+
+                to_scalars(low, 24 if low else high)
+
+            @pl.loop(low, high)
+            def _(i):
+                send_far(g, i)
 
         send_near(g)
 

time: 121 us -> 122 us (level)
    pallas_call x1, Pallas kernels: 119 us -> 120 us  [on_device(): pl.pallas_call(kernel, out_shape=jax.ShapeDtypeStruct((8, TW, TW), bf16),...]
where the time goes in v4:
time: 122 us
  Pallas kernels  120 us (98%)
  local copies, waits for them, and re-layouts  1.67 us (1%)
    pallas_call x1, Pallas kernels, on_device(): pl.pallas_call(kernel, out_shape=jax.ShapeDtypeStruct((8, TW, TW), bf16),...  120 us

profile of v4, /device:TPU:1, one launch (start us, length us, event | category | flops | bytes accessed | tf_op | source)
XLA Modules:
  0.0 122.0 jit_solution(6705700185694460716)
XLA Ops:
  0.0 120.3 %shard_map.64 = bf16[8,128,128]{2,1,0:T(8,128)(2,1)} custom-call(s32[2,32]{1,0:T(2,128)} %lists_ref.1, s32[2]{0:T(128)} %count_ref.1, s32[2,6]{1,0:T(2,128)} %dom_ref.1, s32[2,4]{1,0:T(2,128)} %pair_ref.1, bf16[2,64,128,128]{3,2,1,0:T(8,128)(2,1)} %bitcast.2, bf16[256,10240]{1,0:T(8,128)(2,1)} %orbitals_ref.1), custom_call_target="tpu_custom_call" | custom-call | tf_op jit(solution)/shard_map/pallas_call | solution.py:516
  120.3 1.7 %copy.8 = bf16[2,4,128,128]{3,2,1,0:T(8,128)(2,1)} copy(bf16[2,4,128,128]{3,2,1,0:T(8,128)(2,1)} %bitcast.3) | data formatting | bytes 524288
